TPU v7x, 32 devices: a whole 2x2x4 slice. The times are simulated.
32 devices in a mesh: gx: 4 (over y, core), gy: 8 (over z, x).
Axes of the slice: x: 2, y: 2, z: 4, core: 2. Of those that a mesh axis runs over, the one named last changes fastest.
Arguments:
- x_block: float32 [16, 32, 64, 128], P(None, 'gx', 'gy'), may hold values from -8 to 8
- old_direction: float32 [16, 32, 64, 128], P(None, 'gx', 'gy'), may hold values from -6 to 6
- conductivity: float32 [32, 64, 128], P('gx', 'gy'), may hold values from 0.5 to 4
- fsai_diagonal: float32 [32, 64, 128], P('gx', 'gy'), may hold values from 0.2 to 0.6
- fsai_lower: float32 [13, 32, 64, 128], P(None, 'gx', 'gy'), may hold values from -0.9 to 0.9
- pattern: int32 [8, 13], replicated, may hold values 0 or 1
- step_size: float32 [16], replicated, may hold values from 0.3 to 1.5
- momentum: float32 [16], replicated, may hold values from 0.2 to 1
Outputs:
- x_next: float32 [16, 32, 64, 128], P(None, 'gx', 'gy')
- direction: float32 [16, 32, 64, 128], P(None, 'gx', 'gy')
- rayleigh: float32 [16, 16], replicated
All inputs are finite; a program needn't handle non-finite values.
Results may differ from a plain program's by a relative error of at most 0.00018.
Values sent between devices are 32-bit elements; how exact they have to be, the bound alone decides.
A program may use at most 64 MiB of HBM per device.

v0:
```python
import jax
import jax.numpy as jnp
from jax import lax
from jax.sharding import PartitionSpec as P

BLOCKS = 8
lower_offsets = [
    (a, b, c) for a in (-1, 0, 1) for b in (-1, 0, 1) for c in (-1, 0, 1) if (a, b, c) < (0, 0, 0)
]
face_offsets = [(1, 0, 0), (-1, 0, 0), (0, 1, 0), (0, -1, 0), (0, 0, 1), (0, 0, -1)]


def extended(cells, sides, width):
    for axis, dim in sides:
        count = lax.axis_size(axis)
        ends = count - 1
        head = lax.slice_in_dim(cells, 0, width, axis=dim)
        tail = lax.slice_in_dim(cells, cells.shape[dim] - width, cells.shape[dim], axis=dim)
        cells = jnp.concatenate(
            [
                lax.ppermute(tail, axis, [(i, (i + 1) % count) for i in range(ends)]),
                cells,
                lax.ppermute(head, axis, [((i + 1) % count, i) for i in range(ends)]),
            ],
            axis=dim,
        )
    return cells


def passed_along(array, axis, by):
    size = lax.axis_size(axis)
    pairs = [(i, i + by) for i in range(size) if 0 <= i + by < size]
    return lax.ppermute(array, axis, pairs)


def window(padded, step_x, step_y, step_z, region):
    size_x, size_y, size_z = region
    return padded[
        ...,
        1 + step_x : 1 + step_x + size_x,
        1 + step_y : 1 + step_y + size_y,
        1 + step_z : 1 + step_z + size_z,
    ]


def apply_stiffness(padded, kappa_pad, region):
    centre = window(padded, 0, 0, 0, region)
    kappa_here = window(kappa_pad, 0, 0, 0, region)
    summed = jnp.zeros(centre.shape, jnp.float32)
    for step_x, step_y, step_z in face_offsets:
        face = 0.5 * (kappa_here + window(kappa_pad, step_x, step_y, step_z, region))
        summed = summed + face * (centre - window(padded, step_x, step_y, step_z, region))
    return summed


def apply_factor(padded, diag_here, lower_here, region):
    summed = diag_here * window(padded, 0, 0, 0, region)
    for index, (step_x, step_y, step_z) in enumerate(lower_offsets):
        summed = summed + lower_here[index] * window(padded, step_x, step_y, step_z, region)
    return summed


def apply_transpose(padded, diag_pad, lower_pad, region):
    summed = window(diag_pad, 0, 0, 0, region) * window(padded, 0, 0, 0, region)
    for index, (step_x, step_y, step_z) in enumerate(lower_offsets):
        summed = summed + window(lower_pad[index], -step_x, -step_y, -step_z, region) * window(
            padded, -step_x, -step_y, -step_z, region
        )
    return summed


def pad_depth(field):
    widths = [(0, 0)] * (field.ndim - 1) + [(1, 1)]
    return jnp.pad(field, widths)


def quotient_of(x_block, image, scale):
    local_xx = jnp.sum(x_block * x_block, axis=(1, 2, 3))
    local_xa = jnp.sum(x_block * image, axis=(1, 2, 3))
    sum_xx, sum_xa = lax.psum((local_xx, local_xa), ("gx", "gy"))
    return sum_xa * scale / (sum_xx * scale + 1e-06)


def per_device(
    x_block, old_direction, conductivity, fsai_diagonal, fsai_lower, pattern, step_size, momentum
):
    size_x = x_block.shape[1]
    size_y = x_block.shape[2]
    size_z = x_block.shape[3]
    region = (size_x, size_y, size_z)
    vectors = x_block.shape[0]
    cell_count = size_x * size_y * size_z * lax.axis_size("gx") * lax.axis_size("gy")
    scale = 1.0 / cell_count
    block_id = jnp.arange(size_z, dtype=jnp.int32) // (size_z // BLOCKS)
    onehot = (block_id[:, None] == jnp.arange(BLOCKS, dtype=jnp.int32)[None, :]).astype(jnp.float32)
    active = jnp.dot(onehot, pattern.astype(jnp.float32), precision=lax.Precision.HIGHEST)
    lower_terms = fsai_lower * jnp.transpose(active)[:, None, None, :]
    fields = jnp.concatenate([conductivity[None], fsai_diagonal[None], lower_terms], axis=0)
    fields_wide = extended(fields, (("gx", 1), ("gy", 2)), 1)
    block_wide = pad_depth(extended(x_block, (("gx", 1), ("gy", 2)), 1))
    fields_pad = pad_depth(fields_wide)
    kappa_pad = fields_pad[0]
    diag_pad = fields_pad[1]
    lower_pad = fields_pad[2:]
    image = apply_stiffness(block_wide, kappa_pad, region)
    quotient = quotient_of(x_block, image, scale)
    gradient = image - quotient[:, None, None, None] * x_block
    near_pad = pad_depth(extended(gradient, (("gx", 1), ("gy", 2)), 1))
    product = apply_factor(near_pad, fsai_diagonal, lower_terms, region)
    side_wide = extended(product, (("gy", 2),), 1)
    upper_plane = passed_along(side_wide[:, :1], "gx", -1)
    lower_plane = jnp.zeros(upper_plane.shape, jnp.float32)
    product_pad = pad_depth(jnp.concatenate([lower_plane, side_wide, upper_plane], axis=1))
    smoothed = apply_transpose(product_pad, diag_pad, lower_pad, region)
    direction = smoothed + momentum[:, None, None, None] * old_direction
    direction_pad = pad_depth(extended(direction, (("gx", 1), ("gy", 2)), 1))
    direction_image = apply_stiffness(direction_pad, kappa_pad, region)
    advanced = x_block + step_size[:, None, None, None] * direction
    advanced_image = image + step_size[:, None, None, None] * direction_image
    local_gram = jnp.einsum("kxyz,jxyz->kj", advanced, advanced, precision=lax.Precision.HIGHEST)
    local_stiff = jnp.einsum(
        "kxyz,jxyz->kj", advanced, advanced_image, precision=lax.Precision.HIGHEST
    )
    gram_total, stiff_total = lax.psum((local_gram, local_stiff), ("gx", "gy"))
    identity = jnp.eye(vectors, dtype=jnp.float32)
    gram = gram_total * scale + 1e-05 * identity
    stiff = stiff_total * scale
    factor = jnp.linalg.cholesky(gram)
    inverse = jax.scipy.linalg.solve_triangular(factor, identity, lower=True)
    x_next = jnp.einsum("kj,jxyz->kxyz", inverse, advanced, precision=lax.Precision.HIGHEST)
    rayleigh = jnp.dot(
        jnp.dot(inverse, stiff, precision=lax.Precision.HIGHEST),
        jnp.transpose(inverse),
        precision=lax.Precision.HIGHEST,
    )
    return (x_next, direction, rayleigh)


def solution(mesh):
    placed = (
        P(None, "gx", "gy", None),
        P(None, "gx", "gy", None),
        P("gx", "gy", None),
        P("gx", "gy", None),
        P(None, "gx", "gy", None),
        P(),
        P(),
        P(),
    )
    return jax.shard_map(
        per_device,
        mesh=mesh,
        in_specs=placed,
        out_specs=(P(None, "gx", "gy", None), P(None, "gx", "gy", None), P()),
        check_vma=False,
    )
```

profile of v0, /device:TPU:0, one launch (start us, length us, event | category | flops | bytes accessed | tf_op | source)
XLA Modules:
  0.0 178.6 jit_solution(10476219828083600883)
XLA Ops:
  0.6 0.9 convolution_bitcast_fusion.2
  1.6 1.1 broadcast_multiply_fusion
  2.7 0.7 pad_maximum_fusion.38
  3.5 2.4 %collective-permute-start = (f32[15,1,8,128]{3,2,1,0:T(8,128)S(1)}, f32[15,1,8,128]{3,2,1,0:T(8,128)S(1)}, u32[]{:S(2)}, u32[]{:S(2)}) collective-permute-start(f32[15,1,8,128]{3,2,1,0:T(8,128)S(1)} %get-tuple-element.49), channel_id=1, source_target_pairs={{0,8},{8,16},{16,24},{1,9},{9,17},{17,25},{2,10},{10,18},{18,26},{... | collective-permute-start | bytes 184328 | tf_op jit(solution)/shard_map/ppermute | solution.py:21
  5.8 1.3 collective-permute-start.1
  7.5 5.2 %collective-permute-start.5 = (f32[16,1,8,128]{3,0,2,1:T(8,128)S(1)}, f32[16,1,8,128]{3,0,2,1:T(8,128)S(1)}, u32[]{:S(2)}, u32[]{:S(2)}) collective-permute-start(f32[16,1,8,128]{3,0,2,1:T(8,128)S(1)} %get-tuple-element.48), channel_id=1, source_target_pairs={{0,8},{8,16},{16,24},{1,9},{9,17},{17,25},{2,10},{10,18},{18,26},{... | collective-permute-start | bytes 196616 | tf_op jit(solution)/shard_map/ppermute | solution.py:21
  12.6 1.3 collective-permute-start.4
  14.3 3.4 %collective-permute-start.2 = (f32[15,10,1,128]{3,0,2,1:T(8,128)S(1)}, f32[15,10,1,128]{3,0,2,1:T(8,128)S(1)}, u32[]{:S(2)}, u32[]{:S(2)}) collective-permute-start(f32[15,10,1,128]{3,0,2,1:T(8,128)S(1)} %copy.35), channel_id=1, source_target_pairs={{0,1},{1,2},{2,3},{3,4},{4,5},{5,6},{6,7},{8,9},{9,10},{10,11},{11... | collective-permute-start | bytes 230408 | tf_op jit(solution)/shard_map/ppermute | solution.py:21
  17.7 1.3 collective-permute-start.3
  19.4 1.3 collective-permute-start.6
  20.7 5.2 %collective-permute-start.7 = (f32[16,10,1,128]{3,0,2,1:T(8,128)S(1)}, f32[16,10,1,128]{3,0,2,1:T(8,128)S(1)}, u32[]{:S(2)}, u32[]{:S(2)}) collective-permute-start(f32[16,10,1,128]{3,0,2,1:T(8,128)S(1)} %get-tuple-element.37), channel_id=1, source_target_pairs={{0,1},{1,2},{2,3},{3,4},{4,5},{5,6},{6,7},{8,9},{9,10},{10,11},{11... | collective-permute-start | bytes 245768 | tf_op jit(solution)/shard_map/ppermute | solution.py:21
  26.1 2.8 %select_maximum_fusion = f32[15,10,10,130]{3,2,1,0:T(8,128)S(1)} fusion(f32[15,10,1,128]{3,2,1,0:T(1,128)S(1)} %copy.38, f32[15,10,1,128]{3,2,1,0:T(1,128)S(1)} %copy.37, f32[15,1,8,128]{3,2,1,0:T(8,128)S(1)} %collective-permute-done.1, f32[15,1,8,128]{3,2,1,0:T(8,128)S(1)} %collective-permute-done, f32[13,8,8,128]{3,2,1,0:T(8,128)S(1)} %broadcast_multiply_fusion, ...), kind=kLoop, calls=%fused_computation.13 | loop fusion | flops 3120000 | bytes 1548000 | tf_op jit(solution)/shard_map/concatenate | solution.py:19
  28.9 1.0 slice_bitcast_fusion.14
  30.6 0.8 multiply_reduce_fusion.1
  31.4 44.4 %all-reduce.6 = (f32[16]{0:T(128)S(1)}, f32[16]{0:T(128)S(1)}) all-reduce(f32[16]{0:T(128)S(1)} %multiply_reduce_fusion, f32[16]{0:T(128)S(1)} %get-tuple-element.16), channel_id=1, replica_groups=mesh['gx'=4,'gy'=8] {'gx','gy'}, use_global_device_ids=true, to_apply=%region_3.4 | all-reduce | flops 32 | bytes 256 | tf_op jit(solution)/shard_map/psum | solution.py:80
  76.2 1.3 collective-permute-start.8
  77.5 1.3 collective-permute-start.9
  78.8 4.3 %collective-permute-done.9 = f32[16,1,8,128]{3,0,2,1:T(8,128)S(1)} collective-permute-done((f32[16,1,8,128]{3,0,2,1:T(8,128)S(1)}, f32[16,1,8,128]{3,0,2,1:T(8,128)S(1)}, u32[]{:S(2)}, u32[]{:S(2)}) %collective-permute-start.9) | collective-permute-done | bytes 65568 | tf_op jit(solution)/shard_map/ppermute | solution.py:23
  83.1 2.5 %collective-permute-start.10 = (f32[16,10,1,128]{3,0,2,1:T(8,128)S(1)}, f32[16,10,1,128]{3,0,2,1:T(8,128)S(1)}, u32[]{:S(2)}, u32[]{:S(2)}) collective-permute-start(f32[16,10,1,128]{3,0,2,1:T(8,128)S(1)} %get-tuple-element.35), channel_id=1, source_target_pairs={{0,1},{1,2},{2,3},{3,4},{4,5},{5,6},{6,7},{8,9},{9,10},{10,11},{11... | collective-permute-start | bytes 245768 | tf_op jit(solution)/shard_map/ppermute | solution.py:21
  85.7 1.3 collective-permute-start.11
  87.0 0.7 collective-permute-done.10
  87.8 4.3 %collective-permute-done.11 = f32[16,10,1,128]{3,0,2,1:T(8,128)S(1)} collective-permute-done((f32[16,10,1,128]{3,0,2,1:T(8,128)S(1)}, f32[16,10,1,128]{3,0,2,1:T(8,128)S(1)}, u32[]{:S(2)}, u32[]{:S(2)}) %collective-permute-start.11) | collective-permute-done | bytes 81952 | tf_op jit(solution)/shard_map/ppermute | solution.py:23
  92.5 0.8 fusion.53
  93.4 3.9 %collective-permute-start.12 = (f32[16,8,1,128]{3,0,2,1:T(8,128)S(1)}, f32[16,8,1,128]{3,0,2,1:T(8,128)S(1)}, u32[]{:S(2)}, u32[]{:S(2)}) collective-permute-start(f32[16,8,1,128]{3,0,2,1:T(8,128)S(1)} %get-tuple-element.43), channel_id=1, source_target_pairs={{0,1},{1,2},{2,3},{3,4},{4,5},{5,6},{6,7},{8,9},{9,10},{10,11},{11... | collective-permute-start | bytes 196616 | tf_op jit(solution)/shard_map/ppermute | solution.py:21
  97.3 1.3 collective-permute-start.13
  98.6 0.7 collective-permute-done.12
  99.3 4.6 %collective-permute-done.13 = f32[16,8,1,128]{3,0,2,1:T(8,128)S(1)} collective-permute-done((f32[16,8,1,128]{3,0,2,1:T(8,128)S(1)}, f32[16,8,1,128]{3,0,2,1:T(8,128)S(1)}, u32[]{:S(2)}, u32[]{:S(2)}) %collective-permute-start.13) | collective-permute-done | bytes 65568 | tf_op jit(solution)/shard_map/ppermute | solution.py:23
  103.9 1.3 collective-permute-start.14
  105.2 1.0 slice.508
  106.2 1.0 slice.550
  108.1 0.6 copy-done.2
  108.7 1.3 fusion.16
  110.0 1.3 collective-permute-start.15
  111.3 4.5 %collective-permute-start.16 = (f32[16,1,8,128]{3,0,2,1:T(8,128)S(1)}, f32[16,1,8,128]{3,0,2,1:T(8,128)S(1)}, u32[]{:S(2)}, u32[]{:S(2)}) collective-permute-start(f32[16,1,8,128]{3,0,2,1:T(8,128)S(1)} %get-tuple-element.41), channel_id=1, source_target_pairs={{0,8},{8,16},{16,24},{1,9},{9,17},{17,25},{2,10},{10,18},{18,26},{... | collective-permute-start | bytes 196616 | tf_op jit(solution)/shard_map/ppermute | solution.py:21
  115.8 1.0 copy.56
  116.8 1.3 collective-permute-start.17
  118.1 4.9 %collective-permute-start.18 = (f32[16,10,1,128]{3,0,2,1:T(8,128)S(1)}, f32[16,10,1,128]{3,0,2,1:T(8,128)S(1)}, u32[]{:S(2)}, u32[]{:S(2)}) collective-permute-start(f32[16,10,1,128]{3,0,2,1:T(8,128)S(1)} %get-tuple-element.33), channel_id=1, source_target_pairs={{0,1},{1,2},{2,3},{3,4},{4,5},{5,6},{6,7},{8,9},{9,10},{10,11},{11... | collective-permute-start | bytes 245768 | tf_op jit(solution)/shard_map/ppermute | solution.py:21
  123.0 1.0 convolution_bitcast_fusion.1
  124.0 1.9 %collective-permute-done.18 = f32[16,10,1,128]{3,0,2,1:T(8,128)S(1)} collective-permute-done((f32[16,10,1,128]{3,0,2,1:T(8,128)S(1)}, f32[16,10,1,128]{3,0,2,1:T(8,128)S(1)}, u32[]{:S(2)}, u32[]{:S(2)}) %collective-permute-start.18) | collective-permute-done | bytes 81952 | tf_op jit(solution)/shard_map/ppermute | solution.py:21
  126.5 1.4 convolution_bitcast_fusion
  127.8 43.8 %all-reduce.5 = (f32[16,16]{1,0:T(8,128)S(1)}, f32[16,16]{1,0:T(8,128)S(1)}) all-reduce(f32[16,16]{1,0:T(8,128)S(1)} %convolution_bitcast_fusion.1, f32[16,16]{1,0:T(8,128)S(1)} %convolution_bitcast_fusion), channel_id=1, replica_groups=mesh['gx'=4,'gy'=8] {'gx','gy'}, use_global_device_ids=true, to_apply=%region_4.5 | all-reduce | flops 512 | bytes 4096 | tf_op jit(solution)/shard_map/psum | solution.py:124
  171.7 1.5 cholesky.17
  173.2 0.6 compare_reduce_fusion
  173.8 0.6 fusion.97
  174.5 1.2 custom-call.7
  175.9 0.9 fusion.98
  176.9 0.7 fusion.118
  177.6 1.0 copy.55
  (96 shorter events, 4.6 us)
Async XLA Ops:
  0.6 6.5 %copy-start = (f32[16,8,8,128]{3,2,1,0:T(8,128)S(1)}, f32[16,8,8,128]{3,2,1,0:T(8,128)}, u32[]{:S(2)}) copy-start(f32[16,8,8,128]{3,2,1,0:T(8,128)} %param.8) | copy-start | bytes 1572868
  1.6 12.6 %copy-start.1 = (f32[8,8,128]{2,1,0:T(8,128)S(1)}, f32[8,8,128]{2,1,0:T(8,128)}, u32[]{:S(2)}) copy-start(f32[8,8,128]{2,1,0:T(8,128)} %param.11) | copy-start | bytes 98308
  1.6 12.6 %copy-start.3 = (f32[8,8,128]{2,1,0:T(8,128)S(1)}, f32[8,8,128]{2,1,0:T(8,128)}, u32[]{:S(2)}) copy-start(f32[8,8,128]{2,1,0:T(8,128)} %param.10) | copy-start | bytes 98308
  3.5 10.7 %collective-permute-start = (f32[15,1,8,128]{3,2,1,0:T(8,128)S(1)}, f32[15,1,8,128]{3,2,1,0:T(8,128)S(1)}, u32[]{:S(2)}, u32[]{:S(2)}) collective-permute-start(f32[15,1,8,128]{3,2,1,0:T(8,128)S(1)} %get-tuple-element.49), channel_id=1, source_target_pairs={{0,8},{8,16},{16,24},{1,9},{9,17},{17,25},{2,10},{10,18},{18,26},{... | collective-permute-start | bytes 184328 | tf_op jit(solution)/shard_map/ppermute | solution.py:21
  5.8 8.3 %collective-permute-start.1 = (f32[15,1,8,128]{3,2,1,0:T(8,128)S(1)}, f32[15,1,8,128]{3,2,1,0:T(8,128)S(1)}, u32[]{:S(2)}, u32[]{:S(2)}) collective-permute-start(f32[15,1,8,128]{3,2,1,0:T(8,128)S(1)} %get-tuple-element.50), channel_id=1, source_target_pairs={{8,0},{16,8},{24,16},{9,1},{17,9},{25,17},{10,2},{18,10},{26,18},{... | collective-permute-start | bytes 184328 | tf_op jit(solution)/shard_map/ppermute | solution.py:23
  7.5 11.6 %collective-permute-start.5 = (f32[16,1,8,128]{3,0,2,1:T(8,128)S(1)}, f32[16,1,8,128]{3,0,2,1:T(8,128)S(1)}, u32[]{:S(2)}, u32[]{:S(2)}) collective-permute-start(f32[16,1,8,128]{3,0,2,1:T(8,128)S(1)} %get-tuple-element.48), channel_id=1, source_target_pairs={{0,8},{8,16},{16,24},{1,9},{9,17},{17,25},{2,10},{10,18},{18,26},{... | collective-permute-start | bytes 196616 | tf_op jit(solution)/shard_map/ppermute | solution.py:21
  12.6 6.7 %collective-permute-start.4 = (f32[16,1,8,128]{3,0,2,1:T(8,128)S(1)}, f32[16,1,8,128]{3,0,2,1:T(8,128)S(1)}, u32[]{:S(2)}, u32[]{:S(2)}) collective-permute-start(f32[16,1,8,128]{3,0,2,1:T(8,128)S(1)} %get-tuple-element.47), channel_id=1, source_target_pairs={{8,0},{16,8},{24,16},{9,1},{17,9},{25,17},{10,2},{18,10},{26,18},{... | collective-permute-start | bytes 196616 | tf_op jit(solution)/shard_map/ppermute | solution.py:23
  14.3 11.6 %collective-permute-start.2 = (f32[15,10,1,128]{3,0,2,1:T(8,128)S(1)}, f32[15,10,1,128]{3,0,2,1:T(8,128)S(1)}, u32[]{:S(2)}, u32[]{:S(2)}) collective-permute-start(f32[15,10,1,128]{3,0,2,1:T(8,128)S(1)} %copy.35), channel_id=1, source_target_pairs={{0,1},{1,2},{2,3},{3,4},{4,5},{5,6},{6,7},{8,9},{9,10},{10,11},{11... | collective-permute-start | bytes 230408 | tf_op jit(solution)/shard_map/ppermute | solution.py:21
  17.7 8.3 %collective-permute-start.3 = (f32[15,10,1,128]{3,0,2,1:T(8,128)S(1)}, f32[15,10,1,128]{3,0,2,1:T(8,128)S(1)}, u32[]{:S(2)}, u32[]{:S(2)}) collective-permute-start(f32[15,10,1,128]{3,0,2,1:T(8,128)S(1)} %copy.36), channel_id=1, source_target_pairs={{1,0},{2,1},{3,2},{4,3},{5,4},{6,5},{7,6},{9,8},{10,9},{11,10},{12... | collective-permute-start | bytes 230408 | tf_op jit(solution)/shard_map/ppermute | solution.py:23
  19.4 10.7 %collective-permute-start.6 = (f32[16,10,1,128]{3,0,2,1:T(8,128)S(1)}, f32[16,10,1,128]{3,0,2,1:T(8,128)S(1)}, u32[]{:S(2)}, u32[]{:S(2)}) collective-permute-start(f32[16,10,1,128]{3,0,2,1:T(8,128)S(1)} %get-tuple-element.38), channel_id=1, source_target_pairs={{1,0},{2,1},{3,2},{4,3},{5,4},{6,5},{7,6},{9,8},{10,9},{11,10},{12... | collective-permute-start | bytes 245768 | tf_op jit(solution)/shard_map/ppermute | solution.py:23
  20.7 9.4 %collective-permute-start.7 = (f32[16,10,1,128]{3,0,2,1:T(8,128)S(1)}, f32[16,10,1,128]{3,0,2,1:T(8,128)S(1)}, u32[]{:S(2)}, u32[]{:S(2)}) collective-permute-start(f32[16,10,1,128]{3,0,2,1:T(8,128)S(1)} %get-tuple-element.37), channel_id=1, source_target_pairs={{0,1},{1,2},{2,3},{3,4},{4,5},{5,6},{6,7},{8,9},{9,10},{10,11},{11... | collective-permute-start | bytes 245768 | tf_op jit(solution)/shard_map/ppermute | solution.py:21
  30.0 1.4 copy-start.4
  30.0 1.3 copy-start.6
  30.1 1.3 copy-start.8
  30.1 1.3 copy-start.10
  30.1 1.3 copy-start.12
  30.1 1.3 copy-start.14
  76.2 2.6 %collective-permute-start.8 = (f32[16,1,8,128]{3,0,2,1:T(8,128)S(1)}, f32[16,1,8,128]{3,0,2,1:T(8,128)S(1)}, u32[]{:S(2)}, u32[]{:S(2)}) collective-permute-start(f32[16,1,8,128]{3,0,2,1:T(8,128)S(1)} %get-tuple-element.45), channel_id=1, source_target_pairs={{0,8},{8,16},{16,24},{1,9},{9,17},{17,25},{2,10},{10,18},{18,26},{... | collective-permute-start | bytes 196616 | tf_op jit(solution)/shard_map/ppermute | solution.py:21
  77.5 5.7 %collective-permute-start.9 = (f32[16,1,8,128]{3,0,2,1:T(8,128)S(1)}, f32[16,1,8,128]{3,0,2,1:T(8,128)S(1)}, u32[]{:S(2)}, u32[]{:S(2)}) collective-permute-start(f32[16,1,8,128]{3,0,2,1:T(8,128)S(1)} %get-tuple-element.46), channel_id=1, source_target_pairs={{8,0},{16,8},{24,16},{9,1},{17,9},{25,17},{10,2},{18,10},{26,18},{... | collective-permute-start | bytes 196616 | tf_op jit(solution)/shard_map/ppermute | solution.py:23
  83.1 4.6 %collective-permute-start.10 = (f32[16,10,1,128]{3,0,2,1:T(8,128)S(1)}, f32[16,10,1,128]{3,0,2,1:T(8,128)S(1)}, u32[]{:S(2)}, u32[]{:S(2)}) collective-permute-start(f32[16,10,1,128]{3,0,2,1:T(8,128)S(1)} %get-tuple-element.35), channel_id=1, source_target_pairs={{0,1},{1,2},{2,3},{3,4},{4,5},{5,6},{6,7},{8,9},{9,10},{10,11},{11... | collective-permute-start | bytes 245768 | tf_op jit(solution)/shard_map/ppermute | solution.py:21
  85.7 6.3 %collective-permute-start.11 = (f32[16,10,1,128]{3,0,2,1:T(8,128)S(1)}, f32[16,10,1,128]{3,0,2,1:T(8,128)S(1)}, u32[]{:S(2)}, u32[]{:S(2)}) collective-permute-start(f32[16,10,1,128]{3,0,2,1:T(8,128)S(1)} %get-tuple-element.36), channel_id=1, source_target_pairs={{1,0},{2,1},{3,2},{4,3},{5,4},{6,5},{7,6},{9,8},{10,9},{11,10},{12... | collective-permute-start | bytes 245768 | tf_op jit(solution)/shard_map/ppermute | solution.py:23
  93.4 5.9 %collective-permute-start.12 = (f32[16,8,1,128]{3,0,2,1:T(8,128)S(1)}, f32[16,8,1,128]{3,0,2,1:T(8,128)S(1)}, u32[]{:S(2)}, u32[]{:S(2)}) collective-permute-start(f32[16,8,1,128]{3,0,2,1:T(8,128)S(1)} %get-tuple-element.43), channel_id=1, source_target_pairs={{0,1},{1,2},{2,3},{3,4},{4,5},{5,6},{6,7},{8,9},{9,10},{10,11},{11... | collective-permute-start | bytes 196616 | tf_op jit(solution)/shard_map/ppermute | solution.py:21
  97.3 6.6 %collective-permute-start.13 = (f32[16,8,1,128]{3,0,2,1:T(8,128)S(1)}, f32[16,8,1,128]{3,0,2,1:T(8,128)S(1)}, u32[]{:S(2)}, u32[]{:S(2)}) collective-permute-start(f32[16,8,1,128]{3,0,2,1:T(8,128)S(1)} %get-tuple-element.44), channel_id=1, source_target_pairs={{1,0},{2,1},{3,2},{4,3},{5,4},{6,5},{7,6},{9,8},{10,9},{11,10},{12... | collective-permute-start | bytes 196616 | tf_op jit(solution)/shard_map/ppermute | solution.py:23
  103.9 4.0 %collective-permute-start.14 = (f32[16,1,10,128]{3,0,2,1:T(8,128)S(1)}, f32[16,1,10,128]{3,0,2,1:T(8,128)S(1)}, u32[]{:S(2)}, u32[]{:S(2)}) collective-permute-start(f32[16,1,10,128]{3,0,2,1:T(8,128)S(1)} %pad_maximum_fusion.26), channel_id=1, source_target_pairs={{8,0},{16,8},{24,16},{9,1},{17,9},{25,17},{10,2},{18,10},{26,18},{... | collective-permute-start | bytes 245768 | tf_op jit(solution)/shard_map/ppermute | solution.py:33
  107.6 1.0 copy-start.2
  107.6 1.0 copy-start.17
  110.0 13.0 %copy-start.16 = (f32[16]{0:T(128)S(1)}, f32[16]{0:T(128)}, u32[]{:S(2)}) copy-start(f32[16]{0:T(128)} %param.14) | copy-start | bytes 196
  110.0 6.7 %collective-permute-start.15 = (f32[16,1,8,128]{3,0,2,1:T(8,128)S(1)}, f32[16,1,8,128]{3,0,2,1:T(8,128)S(1)}, u32[]{:S(2)}, u32[]{:S(2)}) collective-permute-start(f32[16,1,8,128]{3,0,2,1:T(8,128)S(1)} %get-tuple-element.42), channel_id=1, source_target_pairs={{8,0},{16,8},{24,16},{9,1},{17,9},{25,17},{10,2},{18,10},{26,18},{... | collective-permute-start | bytes 196616 | tf_op jit(solution)/shard_map/ppermute | solution.py:23
  111.3 5.4 %collective-permute-start.16 = (f32[16,1,8,128]{3,0,2,1:T(8,128)S(1)}, f32[16,1,8,128]{3,0,2,1:T(8,128)S(1)}, u32[]{:S(2)}, u32[]{:S(2)}) collective-permute-start(f32[16,1,8,128]{3,0,2,1:T(8,128)S(1)} %get-tuple-element.41), channel_id=1, source_target_pairs={{0,8},{8,16},{16,24},{1,9},{9,17},{17,25},{2,10},{10,18},{18,26},{... | collective-permute-start | bytes 196616 | tf_op jit(solution)/shard_map/ppermute | solution.py:21
  116.8 7.2 %collective-permute-start.17 = (f32[16,10,1,128]{3,0,2,1:T(8,128)S(1)}, f32[16,10,1,128]{3,0,2,1:T(8,128)S(1)}, u32[]{:S(2)}, u32[]{:S(2)}) collective-permute-start(f32[16,10,1,128]{3,0,2,1:T(8,128)S(1)} %get-tuple-element.34), channel_id=1, source_target_pairs={{1,0},{2,1},{3,2},{4,3},{5,4},{6,5},{7,6},{9,8},{10,9},{11,10},{12... | collective-permute-start | bytes 245768 | tf_op jit(solution)/shard_map/ppermute | solution.py:23
  118.1 8.3 %copy-start.5 = (f32[8,8,128]{2,1,0:T(8,128)S(1)}, f32[8,8,128]{2,1,0:T(8,128)}, u32[]{:S(2)}) copy-start(f32[8,8,128]{2,1,0:T(8,128)} %copy-done.4) | copy-start | bytes 98308
  118.1 8.3 %copy-start.7 = (f32[8,8,128]{2,1,0:T(8,128)S(1)}, f32[8,8,128]{2,1,0:T(8,128)}, u32[]{:S(2)}) copy-start(f32[8,8,128]{2,1,0:T(8,128)} %copy-done.6) | copy-start | bytes 98308
  118.1 8.3 %copy-start.9 = (f32[8,8,128]{2,1,0:T(8,128)S(1)}, f32[8,8,128]{2,1,0:T(8,128)}, u32[]{:S(2)}) copy-start(f32[8,8,128]{2,1,0:T(8,128)} %copy-done.8) | copy-start | bytes 98308
  118.1 8.3 %copy-start.11 = (f32[8,8,128]{2,1,0:T(8,128)S(1)}, f32[8,8,128]{2,1,0:T(8,128)}, u32[]{:S(2)}) copy-start(f32[8,8,128]{2,1,0:T(8,128)} %copy-done.10) | copy-start | bytes 98308
  118.1 8.3 %copy-start.13 = (f32[8,8,128]{2,1,0:T(8,128)S(1)}, f32[8,8,128]{2,1,0:T(8,128)}, u32[]{:S(2)}) copy-start(f32[8,8,128]{2,1,0:T(8,128)} %copy-done.12) | copy-start | bytes 98308
  118.1 8.3 %copy-start.15 = (f32[8,8,128]{2,1,0:T(8,128)S(1)}, f32[8,8,128]{2,1,0:T(8,128)}, u32[]{:S(2)}) copy-start(f32[8,8,128]{2,1,0:T(8,128)} %copy-done.14) | copy-start | bytes 98308
  118.1 7.8 %collective-permute-start.18 = (f32[16,10,1,128]{3,0,2,1:T(8,128)S(1)}, f32[16,10,1,128]{3,0,2,1:T(8,128)S(1)}, u32[]{:S(2)}, u32[]{:S(2)}) collective-permute-start(f32[16,10,1,128]{3,0,2,1:T(8,128)S(1)} %get-tuple-element.33), channel_id=1, source_target_pairs={{0,1},{1,2},{2,3},{3,4},{4,5},{5,6},{6,7},{8,9},{9,10},{10,11},{11... | collective-permute-start | bytes 245768 | tf_op jit(solution)/shard_map/ppermute | solution.py:21
where the time goes:
time: 180 us; the launch traced here: 179 us
  blocking collectives  88.1 us (49%)
  starting transfers between devices  46.1 us (26%)
  waiting for transfers between devices  16.5 us (9%)
  other arithmetic  14 us (8%)
  local copies, waits for them, and re-layouts  7.16 us (4%)
  matrix products  5.21 us (3%)
    psum x1, blocking collectives, quotient_of(): sum_xx, sum_xa = lax.psum((local_xx, local_xa), ('gx', 'gy'))  44.4 us
    psum x1, blocking collectives, per_device(): gram_total, stiff_total = lax.psum((local_gram, local_stiff), ('gx', 'gy'))  43.8 us
    ppermute x9, starting transfers between devices, extended(): lax.ppermute(tail, axis, [(i, (i + 1) % count) for i in range(ends)])  33.2 us
    ppermute x9, waiting for transfers between devices, extended(): lax.ppermute(head, axis, [((i + 1) % count, i) for i in range(ends)])  13.2 us
    ppermute x9, starting transfers between devices, extended(): lax.ppermute(head, axis, [((i + 1) % count, i) for i in range(ends)])  11.6 us
    concatenate x7, other arithmetic, extended(): jnp.concatenate([lax.ppermute(tail, axis, [(i, (i + 1) % count) for i in...  4.35 us
  transfers between devices with their start and end apart: 19, of which 6 were waited for; matrix products, arithmetic and copies ran while one was open for 5% of the time, Pallas kernels for 0%

commit v1 on v0

--- a/solution.py
+++ b/solution.py
@@ -77,7 +77,7 @@
 def quotient_of(x_block, image, scale):
     local_xx = jnp.sum(x_block * x_block, axis=(1, 2, 3))
     local_xa = jnp.sum(x_block * image, axis=(1, 2, 3))
-    sum_xx, sum_xa = lax.psum((local_xx, local_xa), ("gx", "gy"))
+    sum_xx, sum_xa = lax.psum(lax.psum((local_xx, local_xa), "gy"), "gx")
     return sum_xa * scale / (sum_xx * scale + 1e-06)
 
 

time: 180 us -> 162 us (0.900)
  blocking collectives: 88.1 us -> 73.1 us
  waiting for transfers between devices: 16.5 us -> 14.7 us
    psum x1 -> x2, blocking collectives: 44.4 us -> 29.3 us  [quotient_of(): sum_xx, sum_xa = lax.psum(lax.psum((local_xx, local_xa), 'gy'), 'gx')]
  transfers between devices with their start and end apart: 19 -> 19, of which waited for: 6 -> 6; matrix products, arithmetic and copies ran while one was open for 5% -> 6% of each run, Pallas kernels for 0% -> 0%
where the time goes in v1:
time: 162 us; the launch traced here: 161 us
  blocking collectives  73.1 us (45%)
  starting transfers between devices  45.4 us (28%)
  waiting for transfers between devices  14.7 us (9%)
  other arithmetic  14 us (9%)
  local copies, waits for them, and re-layouts  7.16 us (4%)
  matrix products  5.21 us (3%)
    psum x1, blocking collectives, per_device(): gram_total, stiff_total = lax.psum((local_gram, local_stiff), ('gx', 'gy'))  43.8 us
    ppermute x9, starting transfers between devices, extended(): lax.ppermute(tail, axis, [(i, (i + 1) % count) for i in range(ends)])  32.4 us
    psum x2, blocking collectives, quotient_of(): sum_xx, sum_xa = lax.psum(lax.psum((local_xx, local_xa), 'gy'), 'gx')  29.3 us
    ppermute x9, waiting for transfers between devices, extended(): lax.ppermute(head, axis, [((i + 1) % count, i) for i in range(ends)])  12.2 us
    ppermute x9, starting transfers between devices, extended(): lax.ppermute(head, axis, [((i + 1) % count, i) for i in range(ends)])  11.6 us
    concatenate x7, other arithmetic, extended(): jnp.concatenate([lax.ppermute(tail, axis, [(i, (i + 1) % count) for i in...  4.35 us
  transfers between devices with their start and end apart: 19, of which 6 were waited for; matrix products, arithmetic and copies ran while one was open for 6% of the time, Pallas kernels for 0%

profile of v1, /device:TPU:0, one launch (start us, length us, event | category | flops | bytes accessed | tf_op | source)
XLA Modules:
  0.0 161.0 jit_solution(4566177550763627244)
XLA Ops:
  0.6 0.9 convolution_bitcast_fusion.2
  1.6 1.1 broadcast_multiply_fusion
  2.7 0.7 pad_maximum_fusion.38
  3.5 2.4 %collective-permute-start = (f32[15,1,8,128]{3,2,1,0:T(8,128)S(1)}, f32[15,1,8,128]{3,2,1,0:T(8,128)S(1)}, u32[]{:S(2)}, u32[]{:S(2)}) collective-permute-start(f32[15,1,8,128]{3,2,1,0:T(8,128)S(1)} %get-tuple-element.51), channel_id=1, source_target_pairs={{0,8},{8,16},{16,24},{1,9},{9,17},{17,25},{2,10},{10,18},{18,26},{... | collective-permute-start | bytes 184328 | tf_op jit(solution)/shard_map/ppermute | solution.py:21
  5.8 1.3 collective-permute-start.1
  7.5 5.2 %collective-permute-start.5 = (f32[16,1,8,128]{3,0,2,1:T(8,128)S(1)}, f32[16,1,8,128]{3,0,2,1:T(8,128)S(1)}, u32[]{:S(2)}, u32[]{:S(2)}) collective-permute-start(f32[16,1,8,128]{3,0,2,1:T(8,128)S(1)} %get-tuple-element.50), channel_id=1, source_target_pairs={{0,8},{8,16},{16,24},{1,9},{9,17},{17,25},{2,10},{10,18},{18,26},{... | collective-permute-start | bytes 196616 | tf_op jit(solution)/shard_map/ppermute | solution.py:21
  12.6 1.3 collective-permute-start.4
  14.3 3.4 %collective-permute-start.2 = (f32[15,10,1,128]{3,0,2,1:T(8,128)S(1)}, f32[15,10,1,128]{3,0,2,1:T(8,128)S(1)}, u32[]{:S(2)}, u32[]{:S(2)}) collective-permute-start(f32[15,10,1,128]{3,0,2,1:T(8,128)S(1)} %copy.35), channel_id=1, source_target_pairs={{0,1},{1,2},{2,3},{3,4},{4,5},{5,6},{6,7},{8,9},{9,10},{10,11},{11... | collective-permute-start | bytes 230408 | tf_op jit(solution)/shard_map/ppermute | solution.py:21
  17.7 1.3 collective-permute-start.3
  19.4 1.3 collective-permute-start.6
  20.7 5.2 %collective-permute-start.7 = (f32[16,10,1,128]{3,0,2,1:T(8,128)S(1)}, f32[16,10,1,128]{3,0,2,1:T(8,128)S(1)}, u32[]{:S(2)}, u32[]{:S(2)}) collective-permute-start(f32[16,10,1,128]{3,0,2,1:T(8,128)S(1)} %get-tuple-element.39), channel_id=1, source_target_pairs={{0,1},{1,2},{2,3},{3,4},{4,5},{5,6},{6,7},{8,9},{9,10},{10,11},{11... | collective-permute-start | bytes 245768 | tf_op jit(solution)/shard_map/ppermute | solution.py:21
  26.1 2.8 %select_maximum_fusion = f32[15,10,10,130]{3,2,1,0:T(8,128)S(1)} fusion(f32[15,10,1,128]{3,2,1,0:T(1,128)S(1)} %copy.38, f32[15,10,1,128]{3,2,1,0:T(1,128)S(1)} %copy.37, f32[15,1,8,128]{3,2,1,0:T(8,128)S(1)} %collective-permute-done.1, f32[15,1,8,128]{3,2,1,0:T(8,128)S(1)} %collective-permute-done, f32[13,8,8,128]{3,2,1,0:T(8,128)S(1)} %broadcast_multiply_fusion, ...), kind=kLoop, calls=%fused_computation.13 | loop fusion | flops 3120000 | bytes 1548000 | tf_op jit(solution)/shard_map/concatenate | solution.py:19
  28.9 1.0 slice_bitcast_fusion.14
  30.6 0.8 multiply_reduce_fusion.1
  31.4 22.2 %all-reduce.6 = (f32[16]{0:T(128)S(1)}, f32[16]{0:T(128)S(1)}) all-reduce(f32[16]{0:T(128)S(1)} %multiply_reduce_fusion, f32[16]{0:T(128)S(1)} %get-tuple-element.18), channel_id=1, replica_groups=mesh['gx'=4,'gy'=8] {'gy'}, use_global_device_ids=true, to_apply=%region_4.5 | all-reduce | flops 32 | bytes 256 | tf_op jit(solution)/shard_map/psum | solution.py:80
  53.6 7.1 %all-reduce.7 = (f32[16]{0:T(128)S(1)}, f32[16]{0:T(128)S(1)}) all-reduce(f32[16]{0:T(128)S(1)} %get-tuple-element.14, f32[16]{0:T(128)S(1)} %get-tuple-element.15), channel_id=1, replica_groups=mesh['gx'=4,'gy'=8] {'gx'}, use_global_device_ids=true, to_apply=%region_5.6 | all-reduce | flops 32 | bytes 256 | tf_op jit(solution)/shard_map/psum | solution.py:80
  61.1 2.3 %collective-permute-start.8 = (f32[16,1,8,128]{3,0,2,1:T(8,128)S(1)}, f32[16,1,8,128]{3,0,2,1:T(8,128)S(1)}, u32[]{:S(2)}, u32[]{:S(2)}) collective-permute-start(f32[16,1,8,128]{3,0,2,1:T(8,128)S(1)} %get-tuple-element.47), channel_id=1, source_target_pairs={{0,8},{8,16},{16,24},{1,9},{9,17},{17,25},{2,10},{10,18},{18,26},{... | collective-permute-start | bytes 196616 | tf_op jit(solution)/shard_map/ppermute | solution.py:21
  63.4 1.3 collective-permute-start.9
  64.7 3.3 %collective-permute-done.9 = f32[16,1,8,128]{3,0,2,1:T(8,128)S(1)} collective-permute-done((f32[16,1,8,128]{3,0,2,1:T(8,128)S(1)}, f32[16,1,8,128]{3,0,2,1:T(8,128)S(1)}, u32[]{:S(2)}, u32[]{:S(2)}) %collective-permute-start.9) | collective-permute-done | bytes 65568 | tf_op jit(solution)/shard_map/ppermute | solution.py:23
  68.0 1.3 collective-permute-start.10
  69.4 1.3 collective-permute-start.11
  70.7 0.7 collective-permute-done.10
  71.4 4.3 %collective-permute-done.11 = f32[16,10,1,128]{3,0,2,1:T(8,128)S(1)} collective-permute-done((f32[16,10,1,128]{3,0,2,1:T(8,128)S(1)}, f32[16,10,1,128]{3,0,2,1:T(8,128)S(1)}, u32[]{:S(2)}, u32[]{:S(2)}) %collective-permute-start.11) | collective-permute-done | bytes 81952 | tf_op jit(solution)/shard_map/ppermute | solution.py:23
  76.2 0.8 fusion.53
  77.0 3.6 %collective-permute-start.12 = (f32[16,8,1,128]{3,0,2,1:T(8,128)S(1)}, f32[16,8,1,128]{3,0,2,1:T(8,128)S(1)}, u32[]{:S(2)}, u32[]{:S(2)}) collective-permute-start(f32[16,8,1,128]{3,0,2,1:T(8,128)S(1)} %get-tuple-element.45), channel_id=1, source_target_pairs={{0,1},{1,2},{2,3},{3,4},{4,5},{5,6},{6,7},{8,9},{9,10},{10,11},{11... | collective-permute-start | bytes 196616 | tf_op jit(solution)/shard_map/ppermute | solution.py:21
  80.6 1.3 collective-permute-start.13
  81.9 0.7 collective-permute-done.12
  82.6 4.6 %collective-permute-done.13 = f32[16,8,1,128]{3,0,2,1:T(8,128)S(1)} collective-permute-done((f32[16,8,1,128]{3,0,2,1:T(8,128)S(1)}, f32[16,8,1,128]{3,0,2,1:T(8,128)S(1)}, u32[]{:S(2)}, u32[]{:S(2)}) %collective-permute-start.13) | collective-permute-done | bytes 65568 | tf_op jit(solution)/shard_map/ppermute | solution.py:23
  87.3 1.3 collective-permute-start.14
  88.6 1.0 slice.508
  89.5 1.0 slice.550
  92.0 1.3 fusion.16
  93.4 1.3 collective-permute-start.15
  94.7 4.5 %collective-permute-start.16 = (f32[16,1,8,128]{3,0,2,1:T(8,128)S(1)}, f32[16,1,8,128]{3,0,2,1:T(8,128)S(1)}, u32[]{:S(2)}, u32[]{:S(2)}) collective-permute-start(f32[16,1,8,128]{3,0,2,1:T(8,128)S(1)} %get-tuple-element.43), channel_id=1, source_target_pairs={{0,8},{8,16},{16,24},{1,9},{9,17},{17,25},{2,10},{10,18},{18,26},{... | collective-permute-start | bytes 196616 | tf_op jit(solution)/shard_map/ppermute | solution.py:21
  99.2 1.0 copy.56
  100.1 1.3 collective-permute-start.17
  101.5 4.7 %collective-permute-start.18 = (f32[16,10,1,128]{3,0,2,1:T(8,128)S(1)}, f32[16,10,1,128]{3,0,2,1:T(8,128)S(1)}, u32[]{:S(2)}, u32[]{:S(2)}) collective-permute-start(f32[16,10,1,128]{3,0,2,1:T(8,128)S(1)} %get-tuple-element.35), channel_id=1, source_target_pairs={{0,1},{1,2},{2,3},{3,4},{4,5},{5,6},{6,7},{8,9},{9,10},{10,11},{11... | collective-permute-start | bytes 245768 | tf_op jit(solution)/shard_map/ppermute | solution.py:21
  106.2 1.0 convolution_bitcast_fusion.1
  107.2 1.0 collective-permute-done.18
  108.8 1.4 convolution_bitcast_fusion
  110.1 43.8 %all-reduce.5 = (f32[16,16]{1,0:T(8,128)S(1)}, f32[16,16]{1,0:T(8,128)S(1)}) all-reduce(f32[16,16]{1,0:T(8,128)S(1)} %convolution_bitcast_fusion.1, f32[16,16]{1,0:T(8,128)S(1)} %convolution_bitcast_fusion), channel_id=1, replica_groups=mesh['gx'=4,'gy'=8] {'gx','gy'}, use_global_device_ids=true, to_apply=%region_6.7 | all-reduce | flops 512 | bytes 4096 | tf_op jit(solution)/shard_map/psum | solution.py:124
  154.0 1.5 cholesky.17
  155.5 0.6 compare_reduce_fusion
  156.2 0.6 fusion.97
  156.8 1.2 custom-call.7
  158.2 0.9 fusion.98
  159.3 0.7 fusion.118
  160.0 1.0 copy.55
  (97 shorter events, 5.2 us)
Async XLA Ops:
  0.6 6.5 %copy-start = (f32[16,8,8,128]{3,2,1,0:T(8,128)S(1)}, f32[16,8,8,128]{3,2,1,0:T(8,128)}, u32[]{:S(2)}) copy-start(f32[16,8,8,128]{3,2,1,0:T(8,128)} %param.8) | copy-start | bytes 1572868
  1.6 12.6 %copy-start.1 = (f32[8,8,128]{2,1,0:T(8,128)S(1)}, f32[8,8,128]{2,1,0:T(8,128)}, u32[]{:S(2)}) copy-start(f32[8,8,128]{2,1,0:T(8,128)} %param.11) | copy-start | bytes 98308
  1.6 12.6 %copy-start.3 = (f32[8,8,128]{2,1,0:T(8,128)S(1)}, f32[8,8,128]{2,1,0:T(8,128)}, u32[]{:S(2)}) copy-start(f32[8,8,128]{2,1,0:T(8,128)} %param.10) | copy-start | bytes 98308
  3.5 10.7 %collective-permute-start = (f32[15,1,8,128]{3,2,1,0:T(8,128)S(1)}, f32[15,1,8,128]{3,2,1,0:T(8,128)S(1)}, u32[]{:S(2)}, u32[]{:S(2)}) collective-permute-start(f32[15,1,8,128]{3,2,1,0:T(8,128)S(1)} %get-tuple-element.51), channel_id=1, source_target_pairs={{0,8},{8,16},{16,24},{1,9},{9,17},{17,25},{2,10},{10,18},{18,26},{... | collective-permute-start | bytes 184328 | tf_op jit(solution)/shard_map/ppermute | solution.py:21
  5.8 8.3 %collective-permute-start.1 = (f32[15,1,8,128]{3,2,1,0:T(8,128)S(1)}, f32[15,1,8,128]{3,2,1,0:T(8,128)S(1)}, u32[]{:S(2)}, u32[]{:S(2)}) collective-permute-start(f32[15,1,8,128]{3,2,1,0:T(8,128)S(1)} %get-tuple-element.52), channel_id=1, source_target_pairs={{8,0},{16,8},{24,16},{9,1},{17,9},{25,17},{10,2},{18,10},{26,18},{... | collective-permute-start | bytes 184328 | tf_op jit(solution)/shard_map/ppermute | solution.py:23
  7.5 11.6 %collective-permute-start.5 = (f32[16,1,8,128]{3,0,2,1:T(8,128)S(1)}, f32[16,1,8,128]{3,0,2,1:T(8,128)S(1)}, u32[]{:S(2)}, u32[]{:S(2)}) collective-permute-start(f32[16,1,8,128]{3,0,2,1:T(8,128)S(1)} %get-tuple-element.50), channel_id=1, source_target_pairs={{0,8},{8,16},{16,24},{1,9},{9,17},{17,25},{2,10},{10,18},{18,26},{... | collective-permute-start | bytes 196616 | tf_op jit(solution)/shard_map/ppermute | solution.py:21
  12.6 6.7 %collective-permute-start.4 = (f32[16,1,8,128]{3,0,2,1:T(8,128)S(1)}, f32[16,1,8,128]{3,0,2,1:T(8,128)S(1)}, u32[]{:S(2)}, u32[]{:S(2)}) collective-permute-start(f32[16,1,8,128]{3,0,2,1:T(8,128)S(1)} %get-tuple-element.49), channel_id=1, source_target_pairs={{8,0},{16,8},{24,16},{9,1},{17,9},{25,17},{10,2},{18,10},{26,18},{... | collective-permute-start | bytes 196616 | tf_op jit(solution)/shard_map/ppermute | solution.py:23
  14.3 11.6 %collective-permute-start.2 = (f32[15,10,1,128]{3,0,2,1:T(8,128)S(1)}, f32[15,10,1,128]{3,0,2,1:T(8,128)S(1)}, u32[]{:S(2)}, u32[]{:S(2)}) collective-permute-start(f32[15,10,1,128]{3,0,2,1:T(8,128)S(1)} %copy.35), channel_id=1, source_target_pairs={{0,1},{1,2},{2,3},{3,4},{4,5},{5,6},{6,7},{8,9},{9,10},{10,11},{11... | collective-permute-start | bytes 230408 | tf_op jit(solution)/shard_map/ppermute | solution.py:21
  17.7 8.3 %collective-permute-start.3 = (f32[15,10,1,128]{3,0,2,1:T(8,128)S(1)}, f32[15,10,1,128]{3,0,2,1:T(8,128)S(1)}, u32[]{:S(2)}, u32[]{:S(2)}) collective-permute-start(f32[15,10,1,128]{3,0,2,1:T(8,128)S(1)} %copy.36), channel_id=1, source_target_pairs={{1,0},{2,1},{3,2},{4,3},{5,4},{6,5},{7,6},{9,8},{10,9},{11,10},{12... | collective-permute-start | bytes 230408 | tf_op jit(solution)/shard_map/ppermute | solution.py:23
  19.4 10.7 %collective-permute-start.6 = (f32[16,10,1,128]{3,0,2,1:T(8,128)S(1)}, f32[16,10,1,128]{3,0,2,1:T(8,128)S(1)}, u32[]{:S(2)}, u32[]{:S(2)}) collective-permute-start(f32[16,10,1,128]{3,0,2,1:T(8,128)S(1)} %get-tuple-element.40), channel_id=1, source_target_pairs={{1,0},{2,1},{3,2},{4,3},{5,4},{6,5},{7,6},{9,8},{10,9},{11,10},{12... | collective-permute-start | bytes 245768 | tf_op jit(solution)/shard_map/ppermute | solution.py:23
  20.7 9.4 %collective-permute-start.7 = (f32[16,10,1,128]{3,0,2,1:T(8,128)S(1)}, f32[16,10,1,128]{3,0,2,1:T(8,128)S(1)}, u32[]{:S(2)}, u32[]{:S(2)}) collective-permute-start(f32[16,10,1,128]{3,0,2,1:T(8,128)S(1)} %get-tuple-element.39), channel_id=1, source_target_pairs={{0,1},{1,2},{2,3},{3,4},{4,5},{5,6},{6,7},{8,9},{9,10},{10,11},{11... | collective-permute-start | bytes 245768 | tf_op jit(solution)/shard_map/ppermute | solution.py:21
  30.0 1.4 copy-start.4
  30.0 1.3 copy-start.6
  30.1 1.3 copy-start.8
  30.1 1.3 copy-start.10
  30.1 1.3 copy-start.12
  30.1 1.3 copy-start.14
  61.1 3.6 %collective-permute-start.8 = (f32[16,1,8,128]{3,0,2,1:T(8,128)S(1)}, f32[16,1,8,128]{3,0,2,1:T(8,128)S(1)}, u32[]{:S(2)}, u32[]{:S(2)}) collective-permute-start(f32[16,1,8,128]{3,0,2,1:T(8,128)S(1)} %get-tuple-element.47), channel_id=1, source_target_pairs={{0,8},{8,16},{16,24},{1,9},{9,17},{17,25},{2,10},{10,18},{18,26},{... | collective-permute-start | bytes 196616 | tf_op jit(solution)/shard_map/ppermute | solution.py:21
  63.4 4.6 %collective-permute-start.9 = (f32[16,1,8,128]{3,0,2,1:T(8,128)S(1)}, f32[16,1,8,128]{3,0,2,1:T(8,128)S(1)}, u32[]{:S(2)}, u32[]{:S(2)}) collective-permute-start(f32[16,1,8,128]{3,0,2,1:T(8,128)S(1)} %get-tuple-element.48), channel_id=1, source_target_pairs={{8,0},{16,8},{24,16},{9,1},{17,9},{25,17},{10,2},{18,10},{26,18},{... | collective-permute-start | bytes 196616 | tf_op jit(solution)/shard_map/ppermute | solution.py:23
  68.0 3.3 %collective-permute-start.10 = (f32[16,10,1,128]{3,0,2,1:T(8,128)S(1)}, f32[16,10,1,128]{3,0,2,1:T(8,128)S(1)}, u32[]{:S(2)}, u32[]{:S(2)}) collective-permute-start(f32[16,10,1,128]{3,0,2,1:T(8,128)S(1)} %get-tuple-element.37), channel_id=1, source_target_pairs={{0,1},{1,2},{2,3},{3,4},{4,5},{5,6},{6,7},{8,9},{9,10},{10,11},{11... | collective-permute-start | bytes 245768 | tf_op jit(solution)/shard_map/ppermute | solution.py:21
  69.4 6.3 %collective-permute-start.11 = (f32[16,10,1,128]{3,0,2,1:T(8,128)S(1)}, f32[16,10,1,128]{3,0,2,1:T(8,128)S(1)}, u32[]{:S(2)}, u32[]{:S(2)}) collective-permute-start(f32[16,10,1,128]{3,0,2,1:T(8,128)S(1)} %get-tuple-element.38), channel_id=1, source_target_pairs={{1,0},{2,1},{3,2},{4,3},{5,4},{6,5},{7,6},{9,8},{10,9},{11,10},{12... | collective-permute-start | bytes 245768 | tf_op jit(solution)/shard_map/ppermute | solution.py:23
  77.0 5.6 %collective-permute-start.12 = (f32[16,8,1,128]{3,0,2,1:T(8,128)S(1)}, f32[16,8,1,128]{3,0,2,1:T(8,128)S(1)}, u32[]{:S(2)}, u32[]{:S(2)}) collective-permute-start(f32[16,8,1,128]{3,0,2,1:T(8,128)S(1)} %get-tuple-element.45), channel_id=1, source_target_pairs={{0,1},{1,2},{2,3},{3,4},{4,5},{5,6},{6,7},{8,9},{9,10},{10,11},{11... | collective-permute-start | bytes 196616 | tf_op jit(solution)/shard_map/ppermute | solution.py:21
  80.6 6.6 %collective-permute-start.13 = (f32[16,8,1,128]{3,0,2,1:T(8,128)S(1)}, f32[16,8,1,128]{3,0,2,1:T(8,128)S(1)}, u32[]{:S(2)}, u32[]{:S(2)}) collective-permute-start(f32[16,8,1,128]{3,0,2,1:T(8,128)S(1)} %get-tuple-element.46), channel_id=1, source_target_pairs={{1,0},{2,1},{3,2},{4,3},{5,4},{6,5},{7,6},{9,8},{10,9},{11,10},{12... | collective-permute-start | bytes 196616 | tf_op jit(solution)/shard_map/ppermute | solution.py:23
  87.3 4.0 %collective-permute-start.14 = (f32[16,1,10,128]{3,0,2,1:T(8,128)S(1)}, f32[16,1,10,128]{3,0,2,1:T(8,128)S(1)}, u32[]{:S(2)}, u32[]{:S(2)}) collective-permute-start(f32[16,1,10,128]{3,0,2,1:T(8,128)S(1)} %pad_maximum_fusion.26), channel_id=1, source_target_pairs={{8,0},{16,8},{24,16},{9,1},{17,9},{25,17},{10,2},{18,10},{26,18},{... | collective-permute-start | bytes 245768 | tf_op jit(solution)/shard_map/ppermute | solution.py:33
  91.0 1.0 copy-start.2
  91.0 1.0 copy-start.17
  93.3 12.8 %copy-start.16 = (f32[16]{0:T(128)S(1)}, f32[16]{0:T(128)}, u32[]{:S(2)}) copy-start(f32[16]{0:T(128)} %param.14) | copy-start | bytes 196
  93.4 6.7 %collective-permute-start.15 = (f32[16,1,8,128]{3,0,2,1:T(8,128)S(1)}, f32[16,1,8,128]{3,0,2,1:T(8,128)S(1)}, u32[]{:S(2)}, u32[]{:S(2)}) collective-permute-start(f32[16,1,8,128]{3,0,2,1:T(8,128)S(1)} %get-tuple-element.44), channel_id=1, source_target_pairs={{8,0},{16,8},{24,16},{9,1},{17,9},{25,17},{10,2},{18,10},{26,18},{... | collective-permute-start | bytes 196616 | tf_op jit(solution)/shard_map/ppermute | solution.py:23
  94.7 5.4 %collective-permute-start.16 = (f32[16,1,8,128]{3,0,2,1:T(8,128)S(1)}, f32[16,1,8,128]{3,0,2,1:T(8,128)S(1)}, u32[]{:S(2)}, u32[]{:S(2)}) collective-permute-start(f32[16,1,8,128]{3,0,2,1:T(8,128)S(1)} %get-tuple-element.43), channel_id=1, source_target_pairs={{0,8},{8,16},{16,24},{1,9},{9,17},{17,25},{2,10},{10,18},{18,26},{... | collective-permute-start | bytes 196616 | tf_op jit(solution)/shard_map/ppermute | solution.py:21
  100.1 7.0 %collective-permute-start.17 = (f32[16,10,1,128]{3,0,2,1:T(8,128)S(1)}, f32[16,10,1,128]{3,0,2,1:T(8,128)S(1)}, u32[]{:S(2)}, u32[]{:S(2)}) collective-permute-start(f32[16,10,1,128]{3,0,2,1:T(8,128)S(1)} %get-tuple-element.36), channel_id=1, source_target_pairs={{1,0},{2,1},{3,2},{4,3},{5,4},{6,5},{7,6},{9,8},{10,9},{11,10},{12... | collective-permute-start | bytes 245768 | tf_op jit(solution)/shard_map/ppermute | solution.py:23
  101.4 7.3 %copy-start.5 = (f32[8,8,128]{2,1,0:T(8,128)S(1)}, f32[8,8,128]{2,1,0:T(8,128)}, u32[]{:S(2)}) copy-start(f32[8,8,128]{2,1,0:T(8,128)} %copy-done.4) | copy-start | bytes 98308
  101.4 7.3 %copy-start.7 = (f32[8,8,128]{2,1,0:T(8,128)S(1)}, f32[8,8,128]{2,1,0:T(8,128)}, u32[]{:S(2)}) copy-start(f32[8,8,128]{2,1,0:T(8,128)} %copy-done.6) | copy-start | bytes 98308
  101.5 7.3 %copy-start.9 = (f32[8,8,128]{2,1,0:T(8,128)S(1)}, f32[8,8,128]{2,1,0:T(8,128)}, u32[]{:S(2)}) copy-start(f32[8,8,128]{2,1,0:T(8,128)} %copy-done.8) | copy-start | bytes 98308
  101.5 7.3 %copy-start.11 = (f32[8,8,128]{2,1,0:T(8,128)S(1)}, f32[8,8,128]{2,1,0:T(8,128)}, u32[]{:S(2)}) copy-start(f32[8,8,128]{2,1,0:T(8,128)} %copy-done.10) | copy-start | bytes 98308
  101.5 7.3 %copy-start.13 = (f32[8,8,128]{2,1,0:T(8,128)S(1)}, f32[8,8,128]{2,1,0:T(8,128)}, u32[]{:S(2)}) copy-start(f32[8,8,128]{2,1,0:T(8,128)} %copy-done.12) | copy-start | bytes 98308
  101.5 7.3 %copy-start.15 = (f32[8,8,128]{2,1,0:T(8,128)S(1)}, f32[8,8,128]{2,1,0:T(8,128)}, u32[]{:S(2)}) copy-start(f32[8,8,128]{2,1,0:T(8,128)} %copy-done.14) | copy-start | bytes 98308
  101.5 6.7 %collective-permute-start.18 = (f32[16,10,1,128]{3,0,2,1:T(8,128)S(1)}, f32[16,10,1,128]{3,0,2,1:T(8,128)S(1)}, u32[]{:S(2)}, u32[]{:S(2)}) collective-permute-start(f32[16,10,1,128]{3,0,2,1:T(8,128)S(1)} %get-tuple-element.35), channel_id=1, source_target_pairs={{0,1},{1,2},{2,3},{3,4},{4,5},{5,6},{6,7},{8,9},{9,10},{10,11},{11... | collective-permute-start | bytes 245768 | tf_op jit(solution)/shard_map/ppermute | solution.py:21
